TPU v7x, 32 devices: a whole 2x2x4 slice. The times are simulated.
32 devices in a mesh: groups: 2 (over y), seq: 4 (over z), weight: 4 (over x, core).
Axes of the slice: x: 2, y: 2, z: 4, core: 2. Of those that a mesh axis runs over, the one named last changes fastest.
Arguments:
- tokens: bfloat16 [8, 512, 1536], P(('groups', 'weight'), 'seq'), parts along dimension 0, may hold values from -20 to 20
- upstream_grad: bfloat16 [8, 512, 1536], P(('groups', 'weight'), 'seq'), parts along dimension 0, may hold values from -6 to 6
- norm_gain: float32 [1536], replicated, may hold values from 0.5 to 1.5
- norm_bias: float32 [1536], replicated, may hold values from -3 to 3
- input_codes: bfloat16 [1536, 2304], P('weight'), may hold values from -10 to 10
- input_scales: float32 [12, 18], P('weight'), may hold values from 0.02 to 0.06
- input_bias: float32 [2304], replicated, may hold values from -3 to 3
- output_codes: bfloat16 [768, 1536], replicated, may hold values from -4 to 4
- output_scales: float32 [6, 12], replicated, may hold values from 0.02 to 0.06
- layer_scale: float32 [1536], replicated, may hold values from 0.3 to 3
Outputs:
- input_grad: float32 [8, 512, 1536], P(('groups', 'weight'), 'seq'), parts along dimension 0
There are 2 independent parts, one for each index of `groups`. A program takes and returns all parts, laid end to end along the dimension named above; an argument that names none is the same for every part. Nothing has to cross between parts.
All inputs are finite; a program needn't handle non-finite values.
Results may differ from a plain program's by a relative error of at most 0.024.
Values may be sent and summed in bfloat16 or wider, within the bound.
A program may use at most 128 MiB of HBM per device.

v0:
```python
import math

import jax
import jax.numpy as jnp
from jax import lax
from jax.sharding import PartitionSpec as P

HEADS = 12
HEAD_DIM = 64
QBLOCK = 128
HD = 768


def dequantize(codes, scales):
    expanded = jnp.repeat(jnp.repeat(scales, QBLOCK, axis=0), QBLOCK, axis=1)
    return (codes.astype(jnp.float32) * expanded).astype(jnp.bfloat16)


def normalize(rows, gain, shift):
    mean_value = jnp.mean(rows, axis=-1, keepdims=True)
    centered = rows - mean_value
    variance = jnp.mean(centered * centered, axis=-1, keepdims=True)
    inverse = lax.rsqrt(variance + 1e-06)
    normed = centered * inverse
    return (normed, inverse, (normed * gain + shift).astype(jnp.bfloat16))


def norm_backward(grad_norm, normed, inverse, gain):
    grad_hat = grad_norm * gain
    first_mean = jnp.mean(grad_hat, axis=-1, keepdims=True)
    second_mean = jnp.mean(grad_hat * normed, axis=-1, keepdims=True)
    return inverse * (grad_hat - first_mean - normed * second_mean)


def score_block(queries, head_grads, pair_block):
    row_count = pair_block.shape[0]
    keys_blk = pair_block[:, :HD].reshape(row_count, HEADS, HEAD_DIM)
    values_blk = pair_block[:, HD:].reshape(row_count, HEADS, HEAD_DIM)
    scores = jnp.einsum(
        "qhd,khd->hqk", queries, keys_blk, preferred_element_type=jnp.float32
    ) * HEAD_DIM ** (-0.5)
    dprob = jnp.einsum("qhd,khd->hqk", head_grads, values_blk, preferred_element_type=jnp.float32)
    return (keys_blk, scores, dprob)


def update_stats(statistics, queries, head_grads, pair_rows):
    sub_size = math.gcd(pair_rows.shape[0], 512)

    def visit_block(block_index, running):
        run_max, run_total, run_mix = running
        pair_block = lax.dynamic_slice_in_dim(pair_rows, block_index * sub_size, sub_size, 0)
        keys_blk, scores, dprob = score_block(queries, head_grads, pair_block)
        new_max = jnp.maximum(run_max, jnp.max(scores, axis=-1))
        factor = jnp.exp(run_max - new_max)
        expo = jnp.exp(scores - new_max[..., None])
        return (
            new_max,
            run_total * factor + jnp.sum(expo, axis=-1),
            run_mix * factor + jnp.sum(expo * dprob, axis=-1),
        )

    return lax.fori_loop(0, pair_rows.shape[0] // sub_size, visit_block, statistics)


def block_backward(queries, head_grads, pair_block, log_total, row_delta):
    keys_blk, scores, dprob = score_block(queries, head_grads, pair_block)
    weights = jnp.exp(scores - log_total[..., None])
    prob_weights = weights.astype(jnp.bfloat16)
    dscore = (weights * (dprob - row_delta[..., None])).astype(jnp.bfloat16)
    return (keys_blk, prob_weights, dscore)


def key_terms_from(queries, head_grads, prob_weights, dscore):
    key_part = jnp.einsum(
        "hqk,qhd->khd", dscore, queries, preferred_element_type=jnp.float32
    ) * HEAD_DIM ** (-0.5)
    value_part = jnp.einsum(
        "hqk,qhd->khd", prob_weights, head_grads, preferred_element_type=jnp.float32
    )
    row_count = key_part.shape[0]
    return jnp.concatenate(
        [key_part.reshape(row_count, HD), value_part.reshape(row_count, HD)], axis=1
    )


def query_side(queries, head_grads, keys_values, local_rows):
    seq_rows = local_rows * lax.axis_size("seq")
    start_stats = (
        jnp.full((HEADS, local_rows), -1e30, jnp.float32),
        jnp.zeros((HEADS, local_rows), jnp.float32),
        jnp.zeros((HEADS, local_rows), jnp.float32),
    )
    all_pairs = lax.all_gather(keys_values, "seq", axis=0, tiled=True)
    statistics = update_stats(start_stats, queries, head_grads, all_pairs)
    row_max, row_total, row_mix = statistics
    log_total = row_max + jnp.log(row_total)
    row_delta = row_mix / row_total
    sub_size = math.gcd(seq_rows, 512)
    block_count = seq_rows // sub_size
    empty_query = jnp.zeros((local_rows, HEADS, HEAD_DIM), jnp.float32)

    def backward_step(block_index, running):
        query_grad, buffer = running
        pair_block = lax.dynamic_slice_in_dim(all_pairs, block_index * sub_size, sub_size, 0)
        keys_blk, prob_weights, dscore = block_backward(
            queries, head_grads, pair_block, log_total, row_delta
        )
        query_grad = query_grad + jnp.einsum(
            "hqk,khd->qhd", dscore, keys_blk, preferred_element_type=jnp.float32
        )
        block_terms = key_terms_from(queries, head_grads, prob_weights, dscore)
        buffer = lax.dynamic_update_slice_in_dim(buffer, block_terms, block_index * sub_size, 0)
        return (query_grad, buffer)

    empty_terms = jnp.zeros((seq_rows, 2 * HD), jnp.float32)
    query_grad, buffer = lax.fori_loop(0, block_count, backward_step, (empty_query, empty_terms))
    pair_grads = lax.psum_scatter(
        buffer.astype(jnp.bfloat16), "seq", scatter_dimension=0, tiled=True
    ).astype(jnp.float32)
    return (query_grad, pair_grads)


def local(
    tokens,
    upstream_grad,
    norm_gain,
    norm_bias,
    input_codes,
    input_scales,
    input_bias,
    output_codes,
    output_scales,
    layer_scale,
):
    all_codes, all_scales = (
        lax.all_gather(input_codes.astype(jnp.float32), "weight", axis=0, tiled=True).astype(
            input_codes.dtype
        ),
        lax.all_gather(input_scales, "weight", axis=0, tiled=True),
    )
    input_weight = dequantize(all_codes, all_scales)
    output_weight = dequantize(output_codes, output_scales)
    normed, inverse, norm_out = normalize(tokens[0].astype(jnp.float32), norm_gain, norm_bias)
    projected = (
        jnp.dot(norm_out, input_weight, preferred_element_type=jnp.float32) + input_bias
    ).astype(jnp.bfloat16)
    local_rows = projected.shape[0]
    queries = projected[:, :HD].reshape(local_rows, HEADS, HEAD_DIM)
    keys_values = projected[:, HD:]
    scaled_grad = (upstream_grad[0].astype(jnp.float32) * layer_scale).astype(jnp.bfloat16)
    head_grads = jnp.dot(scaled_grad, output_weight.T, preferred_element_type=jnp.float32).astype(
        jnp.bfloat16
    )
    head_grads = head_grads.reshape(local_rows, HEADS, HEAD_DIM)
    query_grad, pair_grads = query_side(queries, head_grads, keys_values, local_rows)
    query_grad = (query_grad * HEAD_DIM ** (-0.5)).reshape(local_rows, HD)
    grad_proj = jnp.concatenate([query_grad, pair_grads], axis=1).astype(jnp.bfloat16)
    grad_norm = jnp.dot(grad_proj, input_weight.T, preferred_element_type=jnp.float32)
    result = norm_backward(grad_norm, normed, inverse, norm_gain)
    return result[None]


def solution(mesh):
    in_specs = (
        P(("groups", "weight"), "seq", None),
        P(("groups", "weight"), "seq", None),
        P(),
        P(),
        P("weight", None),
        P("weight", None),
        P(),
        P(),
        P(),
        P(),
    )
    out_specs = P(("groups", "weight"), "seq", None)
    return jax.shard_map(local, mesh=mesh, in_specs=in_specs, out_specs=out_specs, check_vma=False)
```

profile of v0, /device:TPU:0, one launch (start us, length us, event | category | flops | bytes accessed | tf_op | source)
XLA Modules:
  0.0 167.3 jit_solution(9870443607912164000)
XLA Ops:
  6.5 4.0 %copy.26 = bf16[384,2304]{0,1:T(8,128)(2,1)} copy(bf16[384,2304]{1,0:T(8,128)(2,1)} %param.14) | data formatting | bytes 3538944 | tf_op args[4]
  10.6 6.1 %all-gather = f32[4,3,18]{2,1,0:T(4,128)S(1)} all-gather(f32[1,3,18]{2,1,0:T(4,128)S(1)} %bitcast.98), channel_id=1, replica_groups=mesh['groups'=2,'seq'=4,'weight'=4] {'weight'}, dimensions={0}, use_global_device_ids=true | all-gather | bytes 1080 | tf_op jit(solution)/shard_map/all_gather | solution.py:139
  17.4 46.7 %all-gather.4.cloned.1.call-done = bf16[1536,2304]{0,1:T(8,128)(2,1)} async-done(((bf16[384,2304]{0,1:T(8,128)(2,1)}), bf16[1536,2304]{0,1:T(8,128)(2,1)}) %all-gather.4.cloned.1.call-update) | async-done | bytes 7077904 | tf_op jit(solution)/shard_map/all_gather | solution.py:136
  64.2 4.4 %fusion = bf16[1536,2304]{0,1:T(8,128)(2,1)S(1)} fusion(f32[1536,18]{0,1:T(8,128)S(1)} %bitcast.95, bf16[1536,2304]{0,1:T(8,128)(2,1)} %all-gather.4.cloned.1.call-done), kind=kLoop, calls=%fused_computation.1 | loop fusion | flops 10616832 | bytes 14266368 | tf_op jit(solution)/shard_map/convert_element_type | solution.py:16
  68.7 2.5 %fusion.2 = bf16[128,2304]{1,0:T(8,128)(2,1)S(1)} fusion(bf16[1536,2304]{0,1:T(8,128)(2,1)S(1)} %fusion, f32[2304]{0:T(1024)S(1)} %copy-done.4, bf16[1,128,1536]{2,1,0:T(8,128)(2,1)S(1)} %copy-done.1, f32[1536]{0:T(1024)S(1)} %copy-done.5, f32[1536]{0:T(1024)S(1)} %copy-done.3, f32[128]{0:T(128)S(1)} %add_rsqrt_fusion, f32[128]{0:T(128)S(1)} %broadcast_multiply_fusion.2), kind=kOutput, calls=%fused_computation.5 | convolution fusion | flops 907739136 | bytes 8083456 | tf_op jit(solution)/shard_map/dot_general | solution.py:145
  71.1 0.4 copy-done
  71.5 0.8 slice.22
  72.6 2.8 %copy.30 = bf16[768,1536]{0,1:T(8,128)(2,1)S(1)} copy(bf16[768,1536]{1,0:T(8,128)(2,1)} %param.17) | data formatting | bytes 4718592 | tf_op args[7]
  75.5 0.5 fusion.1
  75.9 0.5 copy-done.2
  76.5 0.5 convolution_convert_fusion
  77.3 32.3 %all-gather.6.cloned.1.call-done = bf16[512,1536]{1,0:T(8,128)(2,1)} async-done(((bf16[128,1536]{1,0:T(8,128)(2,1)}), bf16[512,1536]{1,0:T(8,128)(2,1)}) %all-gather.6.cloned.1.call-update) | async-done | bytes 1572880 | tf_op jit(solution)/shard_map/all_gather | solution.py:93
  109.6 1.5 fusion.42
  111.6 0.7 multiply_reduce_fusion.1
  112.3 1.3 multiply_reduce_fusion
  113.7 0.8 fusion.9
  114.5 0.9 multiply_convert_fusion
  115.8 1.3 pad_maximum_fusion
  117.1 2.7 %copy.34 = bf16[512,1536]{1,0:T(8,128)(2,1)} copy(bf16[512,1536]{0,1:T(8,128)(2,1)} %pad_maximum_fusion) | data formatting | bytes 3145728
  119.8 0.7 fusion.12
  120.4 33.6 %reduce-scatter.4.cloned.1.call-done = bf16[128,1536]{1,0:T(8,128)(2,1)} async-done(((bf16[512,1536]{1,0:T(8,128)(2,1)}), bf16[128,1536]{1,0:T(8,128)(2,1)}) %reduce-scatter.4.cloned.1.call-update) | async-done | bytes 393232
  154.1 1.2 copy.35
  155.3 4.3 %fusion.41 = (f32[128]{0:T(128)S(1)}, f32[128]{0:T(128)S(1)}, f32[128,1536]{1,0:T(8,128)S(1)}) fusion(f32[128]{0:T(128)S(1)} %add_rsqrt_fusion, f32[128]{0:T(128)S(1)} %broadcast_multiply_fusion.2, bf16[1,128,1536]{2,1,0:T(8,128)(2,1)S(1)} %copy-done.1, f32[1536]{0:T(1024)S(1)} %copy-done.3, bf16[1536,2304]{0,1:T(8,128)(2,1)} %copy-done, ...), kind=kOutput, calls=%fused_computation.62 | convolution fusion | flops 908525312 | bytes 8855552 | tf_op jit(solution)/shard_map/dot_general | solution.py:158
  159.6 1.2 fusion.24
  (44 shorter events, 2.3 us)
Async XLA Ops:
  6.5 4.1 %copy-start.8 = (f32[3,18]{1,0:T(4,128)S(1)}, f32[3,18]{1,0:T(4,128)}, u32[]{:S(2)}) copy-start(f32[3,18]{1,0:T(4,128)} %param.15) | copy-start | bytes 652
  6.5 10.5 %copy-start.1 = (bf16[1,128,1536]{2,1,0:T(8,128)(2,1)S(1)}, bf16[1,128,1536]{2,1,0:T(8,128)(2,1)}, u32[]{:S(2)}) copy-start(bf16[1,128,1536]{2,1,0:T(8,128)(2,1)} %param.10) | copy-start | bytes 1179652
  6.5 57.6 %all-gather.4.cloned.1.call-start = ((), (), s32[]{:S(2)}) async-start(), calls=%async_computation.1 | async-start | bytes 8847360 | tf_op jit(solution)/shard_map/all_gather | solution.py:136
  10.5 99.0 %all-gather.6.cloned.1.call-start = ((), (), s32[]{:S(2)}) async-start(), calls=%async_computation.2 | async-start | bytes 1966080 | tf_op jit(solution)/shard_map/all_gather | solution.py:93
  64.1 4.5 %copy-start.3 = (f32[1536]{0:T(1024)S(1)}, f32[1536]{0:T(1024)}, u32[]{:S(2)}) copy-start(f32[1536]{0:T(1024)} %param.12) | copy-start | bytes 18436
  64.2 4.5 %copy-start.4 = (f32[2304]{0:T(1024)S(1)}, f32[2304]{0:T(1024)}, u32[]{:S(2)}) copy-start(f32[2304]{0:T(1024)} %param.16) | copy-start | bytes 27652
  64.2 4.5 %copy-start.5 = (f32[1536]{0:T(1024)S(1)}, f32[1536]{0:T(1024)}, u32[]{:S(2)}) copy-start(f32[1536]{0:T(1024)} %param.13) | copy-start | bytes 18436
  68.6 2.9 %copy-start = (bf16[1536,2304]{0,1:T(8,128)(2,1)}, bf16[1536,2304]{0,1:T(8,128)(2,1)S(1)}, u32[]{:S(2)}) copy-start(bf16[1536,2304]{0,1:T(8,128)(2,1)S(1)} %fusion) | copy-start | bytes 21233668
  68.6 3.7 %copy-start.7 = (f32[6,12]{1,0:T(8,128)S(1)}, f32[6,12]{1,0:T(8,128)}, u32[]{:S(2)}) copy-start(f32[6,12]{1,0:T(8,128)} %param.18) | copy-start | bytes 868
  72.3 81.7 %reduce-scatter.4.cloned.1.call-start = ((), (), s32[]{:S(2)}) async-start(), calls=%async_computation.3 | async-start | bytes 1966080
  75.5 1.0 copy-start.2
  75.5 1.0 copy-start.6
Sparse Core Ops, SparseCore 0:
  10.7 53.4 all-gather.3
  72.5 37.0 all-gather.5
  119.9 34.1 reduce-scatter.3
where the time goes:
time: 168 us; the launch traced here: 167 us
  waiting for transfers between devices  113 us (67%)
  local copies, waits for them, and re-layouts  15.2 us (9%)
  between operations  13.4 us (8%)
  matrix products  11.1 us (7%)
  other arithmetic  8.71 us (5%)
  blocking collectives  6.11 us (4%)
    all_gather x1, waiting for transfers between devices, local(): lax.all_gather(input_codes.astype(jnp.float32), 'weight', axis=0, tiled=T...  46.7 us
    unnamed x4, waiting for transfers between devices  33.7 us
    all_gather x1, waiting for transfers between devices, query_side(): all_pairs = lax.all_gather(keys_values, 'seq', axis=0, tiled=True)  32.3 us
    unnamed x31, local copies, waits for them, and re-layouts  12.1 us
    all_gather x1, blocking collectives, local(): lax.all_gather(input_scales, 'weight', axis=0, tiled=True)  6.11 us
    convert_element_type x2, other arithmetic, dequantize(): return (codes.astype(jnp.float32) * expanded).astype(jnp.bfloat16)  4.89 us
    dot_general x1, matrix products, local(): jnp.dot(grad_proj, input_weight.T, preferred_element_type=jnp.float32)  4.29 us
  transfers between devices with their start and end apart: 3, of which 3 were waited for; matrix products, arithmetic and copies ran while one was open for 3% of the time, Pallas kernels for 0%

commit v1 on v0

--- a/solution.py
+++ b/solution.py
@@ -1,8 +1,11 @@
+import functools
 import math
 
 import jax
 import jax.numpy as jnp
 from jax import lax
+from jax.experimental import pallas as pl
+from jax.experimental.pallas import tpu as pltpu
 from jax.sharding import PartitionSpec as P
 
 HEADS = 12
@@ -120,7 +123,7 @@
     return (query_grad, pair_grads)
 
 
-def local(
+def general(
     tokens,
     upstream_grad,
     norm_gain,
@@ -160,6 +163,352 @@
     return result[None]
 
 
+WIDTH = 1536
+ROWS = 128
+SHARD = 384
+HALF = 384
+GROUP = 192
+BF16 = jnp.bfloat16
+F32 = jnp.float32
+MESH = pl.DeviceIdType.MESH
+NT = (((1,), (1,)), ((), ()))
+
+
+def fits(mesh):
+    return dict(mesh.shape) == {"groups": 2, "seq": 4, "weight": 4}
+
+
+def fused_kernel(
+    tokens_hbm,
+    upstream_hbm,
+    gain_ref,
+    norm_bias_ref,
+    codes_hbm,
+    in_scales,
+    in_bias_ref,
+    out_codes_hbm,
+    out_scales,
+    layer_scale_ref,
+    out_ref,
+    weight,
+    codes,
+    out_codes,
+    out_weight,
+    tokens,
+    upstream,
+    normed_buf,
+    inverse_buf,
+    norm_out,
+    scaled,
+    packed,
+    gathered,
+    grads,
+    grad_proj,
+    load_sem,
+    w_send,
+    w_recv,
+    a_send,
+    a_recv,
+    g_send,
+    g_recv,
+):
+    g = lax.axis_index("groups")
+    s = lax.axis_index("seq")
+    w = lax.axis_index("weight")
+    core = lax.rem(w, 2)
+    across = lax.rem(w + 2, 4)
+    sibling = w + 1 - 2 * core
+    far_sibling = lax.rem(sibling + 2, 4)
+    near = s // 2
+    far = 1 - near
+    buddy = s + 1 - 2 * lax.rem(s, 2)
+    parity = lax.rem(s, 2)
+
+    def load(index, source, target):
+        copy = pltpu.make_async_copy(source, target, load_sem.at[index])
+        copy.start()
+        return copy
+
+    load_codes = load(0, codes_hbm, codes)
+    load_tokens = load(1, tokens_hbm.at[0], tokens)
+    load_upstream = load(2, upstream_hbm.at[0], upstream)
+    load_out_codes = load(3, out_codes_hbm, out_codes)
+
+    barrier = pltpu.get_barrier_semaphore()
+    peers = [{"weight": across}, {"weight": sibling}, {"groups": 1 - g}]
+    peers += [{"seq": lax.rem(s + k, 4)} for k in (1, 2, 3)]
+    for peer in peers:
+        pl.semaphore_signal(barrier, inc=1, device_id=peer, device_id_type=MESH)
+
+    def half_of(j):
+        return far if j < 3 else near
+
+    def columns_of(j):
+        return pl.ds(pl.multiple_of(768 * (j % 3) + HALF * half_of(j), 128), HALF)
+
+    def dequantize_chunk(j):
+        first = 6 * (j % 3) + 3 * half_of(j)
+        for rb in range(3):
+            for cb in range(3):
+                cols = pl.ds(pl.multiple_of(128 * (first + cb), 128), 128)
+                rows = pl.ds(pl.multiple_of(SHARD * w + 128 * rb, 128), 128)
+                block = codes[128 * rb : 128 * (rb + 1), cols].astype(F32)
+                weight[rows, cols] = (block * in_scales[rb, first + cb]).astype(BF16)
+
+    def weight_copy(kind, j, row, count, peer):
+        part = weight.at[pl.ds(pl.multiple_of(row, 64), count), columns_of(j)]
+        return pltpu.make_async_remote_copy(
+            src_ref=part,
+            dst_ref=part,
+            send_sem=w_send.at[kind, j],
+            recv_sem=w_recv.at[kind, j],
+            device_id=peer,
+            device_id_type=MESH,
+        )
+
+    def x_copy(j, owner):
+        return weight_copy(0, j, SHARD * owner + GROUP * g, GROUP, {"weight": across})
+
+    def y_copy(j, part):
+        return weight_copy(1, j, SHARD * across + GROUP * part, GROUP, {"groups": 1 - g})
+
+    def own_copy(j, owner):
+        return weight_copy(2, j, SHARD * owner, SHARD, {"weight": sibling})
+
+    def passed_copy(j, owner):
+        return weight_copy(3, j, SHARD * owner, SHARD, {"weight": sibling})
+
+    def start_own(j):
+        x_copy(j, w).start()
+        own_copy(j, w).start()
+
+    def exchange(t, dest, send_index, recv_index):
+        return pltpu.make_async_remote_copy(
+            src_ref=packed.at[t, pl.ds(pl.multiple_of(GROUP * dest, 64), GROUP), :],
+            dst_ref=gathered.at[t, s],
+            send_sem=a_send.at[t, send_index],
+            recv_sem=a_recv.at[t, recv_index],
+            device_id={"seq": dest},
+            device_id_type=MESH,
+        )
+
+    def exchange_done(t, source, index):
+        return pltpu.make_async_remote_copy(
+            src_ref=packed.at[t, pl.ds(pl.multiple_of(GROUP * source, 64), GROUP), :],
+            dst_ref=gathered.at[t, source],
+            send_sem=a_send.at[t, index],
+            recv_sem=a_recv.at[t, index],
+            device_id={"seq": source},
+            device_id_type=MESH,
+        )
+
+    def share(t, is_far, value):
+        half = far if is_far else near
+        packed[t, pl.ds(pl.multiple_of(HALF * half, 128), HALF), :] = value
+        if is_far:
+            for k in range(2):
+                exchange(t, 2 * far + k, k, parity).start()
+        else:
+            exchange(t, buddy, 2, 2).start()
+            gathered[t, s] = packed[t, pl.ds(pl.multiple_of(GROUP * s, 64), GROUP), :]
+
+    def head_gradients(is_far):
+        half = far if is_far else near
+        for rb in range(3):
+            rows = pl.ds(pl.multiple_of(HALF * half + 128 * rb, 128), 128)
+            for cb in range(12):
+                block = out_codes[rows, 128 * cb : 128 * (cb + 1)].astype(F32)
+                out_weight[128 * rb : 128 * (rb + 1), 128 * cb : 128 * (cb + 1)] = (
+                    block * out_scales[3 * half + rb, cb]
+                ).astype(BF16)
+        value = lax.dot_general(out_weight[...], scaled[...], NT, preferred_element_type=F32)
+        share(3, is_far, value.astype(BF16))
+
+    def project(j):
+        value = jnp.dot(norm_out[...], weight[:, columns_of(j)], preferred_element_type=F32)
+        value = value + in_bias_ref[:, columns_of(j)]
+        if j % 3 == 0:
+            value = value * HEAD_DIM ** (-0.5)
+        share(j % 3, j < 3, value.T.astype(BF16))
+
+    load_codes.wait()
+    dequantize_chunk(0)
+    dequantize_chunk(1)
+    pl.semaphore_wait(barrier, 6)
+    start_own(0)
+    start_own(1)
+    for j in range(2, 6):
+        dequantize_chunk(j)
+
+    load_upstream.wait()
+    scaled[...] = (upstream[...].astype(F32) * layer_scale_ref[...]).astype(BF16)
+    load_out_codes.wait()
+    head_gradients(True)
+
+    load_tokens.wait()
+    normed, inverse, rounded = normalize(
+        tokens[...].astype(F32), gain_ref[...], norm_bias_ref[...]
+    )
+    normed_buf[...] = normed
+    inverse_buf[...] = inverse
+    norm_out[...] = rounded
+
+    for step in range(8):
+        if step < 6:
+            x_copy(step, across).wait_recv()
+            if step + 2 < 6:
+                start_own(step + 2)
+            y_copy(step, g).start()
+        if 1 <= step < 7:
+            y_copy(step - 1, 1 - g).wait_recv()
+            passed_copy(step - 1, across).start()
+        if step == 0:
+            head_gradients(False)
+        if step >= 2:
+            own_copy(step - 2, sibling).wait_recv()
+            passed_copy(step - 2, far_sibling).wait_recv()
+            project(step - 2)
+
+    for t in (0, 1, 2, 3):
+        for k in range(2):
+            exchange_done(t, 2 * far + k, k).wait_recv()
+        exchange_done(t, buddy, 2).wait_recv()
+
+    def grad_copy(h, dest, source, send_index, recv_index, peer):
+        rows = pl.ds(pl.multiple_of(GROUP * source + HEAD_DIM * h, 64), HEAD_DIM)
+        return pltpu.make_async_remote_copy(
+            src_ref=grads.at[h, dest],
+            dst_ref=grad_proj.at[:, rows, :],
+            send_sem=g_send.at[h, send_index],
+            recv_sem=g_recv.at[h, recv_index],
+            device_id={"seq": peer},
+            device_id_type=MESH,
+        )
+
+    for h in range(3):
+        rows = slice(HEAD_DIM * h, HEAD_DIM * (h + 1))
+        q_t, k_t, v_t, g_t = (
+            jnp.concatenate([gathered[t, i, rows, :] for i in range(4)], axis=1) for t in range(4)
+        )
+        scores = jnp.dot(k_t.T, q_t, preferred_element_type=F32)
+        dprob = jnp.dot(v_t.T, g_t, preferred_element_type=F32)
+        expo = jnp.exp(scores - jnp.max(scores, axis=0, keepdims=True))
+        probs = expo * (1.0 / jnp.sum(expo, axis=0, keepdims=True))
+        delta = jnp.sum(probs * dprob, axis=0, keepdims=True)
+        dscore = (probs * (dprob - delta)).astype(BF16)
+        parts = (
+            jnp.dot(k_t, dscore, preferred_element_type=F32) * HEAD_DIM ** (-0.5),
+            lax.dot_general(q_t, dscore, NT, preferred_element_type=F32),
+            lax.dot_general(g_t, probs.astype(BF16), NT, preferred_element_type=F32),
+        )
+        for t in range(3):
+            value = parts[t].astype(BF16)
+            for i in range(4):
+                grads[h, i, t] = value[:, ROWS * i : ROWS * (i + 1)]
+        for k in range(2):
+            grad_copy(h, 2 * far + k, s, k, parity, 2 * far + k).start()
+        grad_copy(h, buddy, s, 2, 2, buddy).start()
+        own = pl.ds(pl.multiple_of(GROUP * s + HEAD_DIM * h, 64), HEAD_DIM)
+        grad_proj[:, own, :] = grads[h, s]
+
+    def back(half):
+        total = None
+        for t in range(3):
+            rows = pl.ds(pl.multiple_of(HALF * half, 128), HALF)
+            cols = pl.ds(pl.multiple_of(768 * t + HALF * half, 128), HALF)
+            term = lax.dot_general(
+                grad_proj[t, rows, :].T, weight[:, cols], NT, preferred_element_type=F32
+            )
+            total = term if total is None else total + term
+        return total
+
+    for h in range(3):
+        grad_copy(h, buddy, buddy, 2, 2, buddy).wait_recv()
+    out_ref[0] = back(near)
+    for h in range(3):
+        for k in range(2):
+            grad_copy(h, 2 * far + k, 2 * far + k, k, k, 2 * far + k).wait_recv()
+    grad_norm = out_ref[0] + back(far)
+    out_ref[0] = norm_backward(grad_norm, normed_buf[...], inverse_buf[...], gain_ref[...])
+
+    for j in range(6):
+        x_copy(j, w).wait_send()
+        own_copy(j, w).wait_send()
+        y_copy(j, g).wait_send()
+        passed_copy(j, across).wait_send()
+    for t in range(4):
+        for k in range(2):
+            exchange(t, 2 * far + k, k, parity).wait_send()
+        exchange(t, buddy, 2, 2).wait_send()
+    for h in range(3):
+        for k in range(2):
+            grad_copy(h, 2 * far + k, s, k, parity, 2 * far + k).wait_send()
+        grad_copy(h, buddy, s, 2, 2, buddy).wait_send()
+
+
+def fused(
+    tokens,
+    upstream_grad,
+    norm_gain,
+    norm_bias,
+    input_codes,
+    input_scales,
+    input_bias,
+    output_codes,
+    output_scales,
+    layer_scale,
+):
+    anywhere = pl.BlockSpec(memory_space=pl.ANY)
+    vmem = pl.BlockSpec(memory_space=pltpu.VMEM)
+    smem = pl.BlockSpec(memory_space=pltpu.SMEM)
+    return pl.pallas_call(
+        fused_kernel,
+        out_shape=jax.ShapeDtypeStruct((1, ROWS, WIDTH), F32),
+        in_specs=[anywhere, anywhere, vmem, vmem, anywhere, smem, vmem, anywhere, smem, vmem],
+        out_specs=vmem,
+        scratch_shapes=[
+            pltpu.VMEM((WIDTH, 3 * HD), BF16),
+            pltpu.VMEM((SHARD, 3 * HD), BF16),
+            pltpu.VMEM((HD, WIDTH), BF16),
+            pltpu.VMEM((HALF, WIDTH), BF16),
+            pltpu.VMEM((ROWS, WIDTH), BF16),
+            pltpu.VMEM((ROWS, WIDTH), BF16),
+            pltpu.VMEM((ROWS, WIDTH), F32),
+            pltpu.VMEM((ROWS, 1), F32),
+            pltpu.VMEM((ROWS, WIDTH), BF16),
+            pltpu.VMEM((ROWS, WIDTH), BF16),
+            pltpu.VMEM((4, HD, ROWS), BF16),
+            pltpu.VMEM((4, 4, GROUP, ROWS), BF16),
+            pltpu.VMEM((3, 4, 3, HEAD_DIM, ROWS), BF16),
+            pltpu.VMEM((3, HD, ROWS), BF16),
+            pltpu.SemaphoreType.DMA((4,)),
+            pltpu.SemaphoreType.DMA((4, 6)),
+            pltpu.SemaphoreType.DMA((4, 6)),
+            pltpu.SemaphoreType.DMA((4, 3)),
+            pltpu.SemaphoreType.DMA((4, 3)),
+            pltpu.SemaphoreType.DMA((3, 3)),
+            pltpu.SemaphoreType.DMA((3, 3)),
+        ],
+        compiler_params=pltpu.CompilerParams(
+            collective_id=0, has_side_effects=True, vmem_limit_bytes=52 * 1024 * 1024
+        ),
+        cost_estimate=pl.CostEstimate(
+            flops=2500000000, bytes_accessed=8000000, transcendentals=1000000
+        ),
+    )(
+        tokens,
+        upstream_grad,
+        norm_gain[None],
+        norm_bias[None],
+        input_codes,
+        input_scales,
+        input_bias[None],
+        output_codes,
+        output_scales,
+        layer_scale[None],
+    )
+
+
 def solution(mesh):
     in_specs = (
         P(("groups", "weight"), "seq", None),
@@ -174,4 +523,5 @@
         P(),
     )
     out_specs = P(("groups", "weight"), "seq", None)
+    local = fused if fits(mesh) else general
     return jax.shard_map(local, mesh=mesh, in_specs=in_specs, out_specs=out_specs, check_vma=False)

time: 168 us -> 61.8 us (0.37)
  waiting for transfers between devices: 113 us -> 0 us
  Pallas kernels: 0 us -> 54.3 us
  between operations: 13.4 us -> 0.02 us
  matrix products: 11.1 us -> 0 us
  other arithmetic: 8.71 us -> 0 us
  local copies, waits for them, and re-layouts: 15.2 us -> 7.05 us
  blocking collectives: 6.11 us -> 0 us
    all_gather x2 -> x0, waiting for transfers between devices: 79 us -> none  [the longest x1 46.7 us: local(): lax.all_gather(input_codes.astype(jnp.float32), 'weight', axis=0, tiled=T...]
    pallas_call x0 -> x1, Pallas kernels: none -> 54.3 us  [fused(): pl.pallas_call(fused_kernel, out_shape=jax.ShapeDtypeStruct((1, ROWS, WID...]
    unnamed x4 -> x0, waiting for transfers between devices: 33.7 us -> none
    dot_general x8 -> x0, matrix products: 11.1 us -> none  [the longest x1 4.29 us: local(): jnp.dot(grad_proj, input_weight.T, preferred_element_type=jnp.float32)]
    unnamed x31 -> x9, local copies, waits for them, and re-layouts: 12.1 us -> 4.24 us
    all_gather x1 -> x0, blocking collectives: 6.11 us -> none  [local(): lax.all_gather(input_scales, 'weight', axis=0, tiled=True)]
    convert_element_type x3 -> x0, other arithmetic: 5.77 us -> none  [the longest x2 4.89 us: dequantize(): return (codes.astype(jnp.float32) * expanded).astype(jnp.bfloat16)]
    slice x6 -> x0, local copies, waits for them, and re-layouts: 2.98 us -> none  [the longest x2 1.75 us: score_block(): values_blk = pair_block[:, HD:].reshape(row_count, HEADS, HEAD_DIM)]
  transfers between devices with their start and end apart: 3 -> 0, of which waited for: 3 -> 0; matrix products, arithmetic and copies ran while one was open for 3% -> 0% of each run, Pallas kernels for 0% -> 0%
where the time goes in v1:
time: 61.8 us; the launch traced here: 61.4 us
  Pallas kernels  54.3 us (88%)
  local copies, waits for them, and re-layouts  7.05 us (11%)
    pallas_call x1, Pallas kernels, fused(): pl.pallas_call(fused_kernel, out_shape=jax.ShapeDtypeStruct((1, ROWS, WID...  54.3 us
    unnamed x9, local copies, waits for them, and re-layouts  4.24 us

profile of v1, /device:TPU:0, one launch (start us, length us, event | category | flops | bytes accessed | tf_op | source)
XLA Modules:
  0.0 61.4 jit_solution(1585085864842174598)
XLA Ops:
  0.0 0.7 %broadcast_in_dim.12.gain_ref = f32[1,1536]{1,0:T(1,128)S(1)} reshape(f32[1536]{0:T(1024)} %param.12) | data formatting | bytes 12288 | tf_op jit(solution)/shard_map/broadcast_in_dim | solution.py:501
  0.7 0.7 %broadcast_in_dim.13.norm_bias_ref = f32[1,1536]{1,0:T(1,128)S(1)} reshape(f32[1536]{0:T(1024)} %param.13) | data formatting | bytes 12288 | tf_op jit(solution)/shard_map/broadcast_in_dim | solution.py:502
  1.4 0.7 %broadcast_in_dim.15.layer_scale_ref = f32[1,1536]{1,0:T(1,128)S(1)} reshape(f32[1536]{0:T(1024)} %param.19) | data formatting | bytes 12288 | tf_op jit(solution)/shard_map/broadcast_in_dim | solution.py:508
  2.1 0.7 %broadcast_in_dim.14.in_bias_ref = f32[1,2304]{1,0:T(1,128)S(1)} reshape(f32[2304]{0:T(1024)} %param.16) | data formatting | bytes 18432 | tf_op jit(solution)/shard_map/broadcast_in_dim | solution.py:505
  2.8 0.0 copy-start
  2.8 1.0 %copy-done = bf16[1,128,1536]{2,1,0:T(8,128)(2,1)S(1)} copy-done((bf16[1,128,1536]{2,1,0:T(8,128)(2,1)S(1)}, bf16[1,128,1536]{2,1,0:T(8,128)(2,1)}, u32[]{:S(2)}) %copy-start) | copy-done | bytes 393240
  3.8 0.0 copy-start.1
  3.8 1.0 %copy-done.1 = bf16[1,128,1536]{2,1,0:T(8,128)(2,1)S(1)} copy-done((bf16[1,128,1536]{2,1,0:T(8,128)(2,1)S(1)}, bf16[1,128,1536]{2,1,0:T(8,128)(2,1)}, u32[]{:S(2)}) %copy-start.1) | copy-done | bytes 393240
  4.8 0.0 copy-start.2
  4.8 0.7 %copy-done.2 = f32[6,12]{1,0:T(8,128)S(1)} copy-done((f32[6,12]{1,0:T(8,128)S(1)}, f32[6,12]{1,0:T(8,128)}, u32[]{:S(2)}) %copy-start.2) | copy-done | bytes 312
  5.5 0.0 copy-start.3
  5.5 0.7 %copy-done.3 = f32[3,18]{1,0:T(4,128)S(1)} copy-done((f32[3,18]{1,0:T(4,128)S(1)}, f32[3,18]{1,0:T(4,128)}, u32[]{:S(2)}) %copy-start.3) | copy-done | bytes 240
  6.2 54.3 %shard_map.100 = f32[1,128,1536]{2,1,0:T(8,128)S(1)} custom-call(bf16[1,128,1536]{2,1,0:T(8,128)(2,1)S(1)} %copy-done, bf16[1,128,1536]{2,1,0:T(8,128)(2,1)S(1)} %copy-done.1, f32[1,1536]{1,0:T(1,128)S(1)} %broadcast_in_dim.12.gain_ref, f32[1,1536]{1,0:T(1,128)S(1)} %broadcast_in_dim.13.norm_bias_ref, bf16[384,2304]{1,0:T(8,128)(2,1)} %codes_hbm.1, ...), custom_call_target="tpu_custom_call" | custom-call | flops 2500000000 | bytes 8000000 | tf_op jit(solution)/shard_map/pallas_call | solution.py:464
  60.5 0.9 %copy.12 = f32[1,128,1536]{2,1,0:T(8,128)} copy(f32[1,128,1536]{2,1,0:T(8,128)S(1)} %shard_map.100) | data formatting | bytes 1572864
Async XLA Ops:
  2.8 1.0 %copy-start = (bf16[1,128,1536]{2,1,0:T(8,128)(2,1)S(1)}, bf16[1,128,1536]{2,1,0:T(8,128)(2,1)}, u32[]{:S(2)}) copy-start(bf16[1,128,1536]{2,1,0:T(8,128)(2,1)} %tokens_hbm.1) | copy-start | bytes 1179652
  3.8 1.0 %copy-start.1 = (bf16[1,128,1536]{2,1,0:T(8,128)(2,1)S(1)}, bf16[1,128,1536]{2,1,0:T(8,128)(2,1)}, u32[]{:S(2)}) copy-start(bf16[1,128,1536]{2,1,0:T(8,128)(2,1)} %upstream_hbm.1) | copy-start | bytes 1179652
  4.8 0.7 %copy-start.2 = (f32[6,12]{1,0:T(8,128)S(1)}, f32[6,12]{1,0:T(8,128)}, u32[]{:S(2)}) copy-start(f32[6,12]{1,0:T(8,128)} %out_scales.1) | copy-start | bytes 868
  5.5 0.7 %copy-start.3 = (f32[3,18]{1,0:T(4,128)S(1)}, f32[3,18]{1,0:T(4,128)}, u32[]{:S(2)}) copy-start(f32[3,18]{1,0:T(4,128)} %in_scales.1) | copy-start | bytes 652

commit v2 on v1

--- a/solution.py
+++ b/solution.py
@@ -181,15 +181,21 @@
 def fused_kernel(
     tokens_hbm,
     upstream_hbm,
+    gain_hbm,
+    norm_bias_hbm,
+    codes_hbm,
+    in_scales_hbm,
+    in_bias_hbm,
+    out_codes_hbm,
+    out_scales_hbm,
+    layer_scale_hbm,
+    out_ref,
     gain_ref,
     norm_bias_ref,
-    codes_hbm,
     in_scales,
     in_bias_ref,
-    out_codes_hbm,
     out_scales,
     layer_scale_ref,
-    out_ref,
     weight,
     codes,
     out_codes,
@@ -229,10 +235,16 @@
         copy.start()
         return copy
 
+    load_in_scales = load(4, in_scales_hbm, in_scales)
     load_codes = load(0, codes_hbm, codes)
     load_tokens = load(1, tokens_hbm.at[0], tokens)
     load_upstream = load(2, upstream_hbm.at[0], upstream)
     load_out_codes = load(3, out_codes_hbm, out_codes)
+    load_out_scales = load(5, out_scales_hbm, out_scales)
+    load_layer_scale = load(6, layer_scale_hbm, layer_scale_ref)
+    load_gain = load(7, gain_hbm, gain_ref)
+    load_norm_bias = load(8, norm_bias_hbm, norm_bias_ref)
+    load_in_bias = load(9, in_bias_hbm, in_bias_ref)
 
     barrier = pltpu.get_barrier_semaphore()
     peers = [{"weight": across}, {"weight": sibling}, {"groups": 1 - g}]
@@ -326,11 +338,12 @@
 
     def project(j):
         value = jnp.dot(norm_out[...], weight[:, columns_of(j)], preferred_element_type=F32)
-        value = value + in_bias_ref[:, columns_of(j)]
+        value = value + in_bias_ref[columns_of(j)][None]
         if j % 3 == 0:
             value = value * HEAD_DIM ** (-0.5)
         share(j % 3, j < 3, value.T.astype(BF16))
 
+    load_in_scales.wait()
     load_codes.wait()
     dequantize_chunk(0)
     dequantize_chunk(1)
@@ -340,14 +353,19 @@
     for j in range(2, 6):
         dequantize_chunk(j)
 
+    load_layer_scale.wait()
     load_upstream.wait()
-    scaled[...] = (upstream[...].astype(F32) * layer_scale_ref[...]).astype(BF16)
+    scaled[...] = (upstream[...].astype(F32) * layer_scale_ref[...][None]).astype(BF16)
+    load_out_scales.wait()
     load_out_codes.wait()
     head_gradients(True)
 
+    load_gain.wait()
+    load_norm_bias.wait()
+    load_in_bias.wait()
     load_tokens.wait()
     normed, inverse, rounded = normalize(
-        tokens[...].astype(F32), gain_ref[...], norm_bias_ref[...]
+        tokens[...].astype(F32), gain_ref[...][None], norm_bias_ref[...][None]
     )
     normed_buf[...] = normed
     inverse_buf[...] = inverse
@@ -429,7 +447,7 @@
         for k in range(2):
             grad_copy(h, 2 * far + k, 2 * far + k, k, k, 2 * far + k).wait_recv()
     grad_norm = out_ref[0] + back(far)
-    out_ref[0] = norm_backward(grad_norm, normed_buf[...], inverse_buf[...], gain_ref[...])
+    out_ref[0] = norm_backward(grad_norm, normed_buf[...], inverse_buf[...], gain_ref[...][None])
 
     for j in range(6):
         x_copy(j, w).wait_send()
@@ -458,15 +476,20 @@
     output_scales,
     layer_scale,
 ):
-    anywhere = pl.BlockSpec(memory_space=pl.ANY)
+    hbm = pl.BlockSpec(memory_space=pltpu.HBM)
     vmem = pl.BlockSpec(memory_space=pltpu.VMEM)
-    smem = pl.BlockSpec(memory_space=pltpu.SMEM)
     return pl.pallas_call(
         fused_kernel,
         out_shape=jax.ShapeDtypeStruct((1, ROWS, WIDTH), F32),
-        in_specs=[anywhere, anywhere, vmem, vmem, anywhere, smem, vmem, anywhere, smem, vmem],
+        in_specs=[hbm] * 10,
         out_specs=vmem,
         scratch_shapes=[
+            pltpu.VMEM((WIDTH,), F32),
+            pltpu.VMEM((WIDTH,), F32),
+            pltpu.SMEM((3, 18), F32),
+            pltpu.VMEM((3 * HD,), F32),
+            pltpu.SMEM((6, 12), F32),
+            pltpu.VMEM((WIDTH,), F32),
             pltpu.VMEM((WIDTH, 3 * HD), BF16),
             pltpu.VMEM((SHARD, 3 * HD), BF16),
             pltpu.VMEM((HD, WIDTH), BF16),
@@ -481,7 +504,7 @@
             pltpu.VMEM((4, 4, GROUP, ROWS), BF16),
             pltpu.VMEM((3, 4, 3, HEAD_DIM, ROWS), BF16),
             pltpu.VMEM((3, HD, ROWS), BF16),
-            pltpu.SemaphoreType.DMA((4,)),
+            pltpu.SemaphoreType.DMA((10,)),
             pltpu.SemaphoreType.DMA((4, 6)),
             pltpu.SemaphoreType.DMA((4, 6)),
             pltpu.SemaphoreType.DMA((4, 3)),
@@ -490,7 +513,7 @@
             pltpu.SemaphoreType.DMA((3, 3)),
         ],
         compiler_params=pltpu.CompilerParams(
-            collective_id=0, has_side_effects=True, vmem_limit_bytes=52 * 1024 * 1024
+            collective_id=0, has_side_effects=True, vmem_limit_bytes=64 * 1024 * 1024 - 65536
         ),
         cost_estimate=pl.CostEstimate(
             flops=2500000000, bytes_accessed=8000000, transcendentals=1000000
@@ -498,14 +521,14 @@
     )(
         tokens,
         upstream_grad,
-        norm_gain[None],
-        norm_bias[None],
+        norm_gain,
+        norm_bias,
         input_codes,
         input_scales,
-        input_bias[None],
+        input_bias,
         output_codes,
         output_scales,
-        layer_scale[None],
+        layer_scale,
     )
 
 

time: 61.8 us -> 56.7 us (0.917)
  local copies, waits for them, and re-layouts: 7.05 us -> 2.07 us
    broadcast_in_dim x4 -> x0, local copies, waits for them, and re-layouts: 2.82 us -> none  [the longest x1 0.71 us: fused(): input_bias[None]]
    unnamed x9 -> x1, local copies, waits for them, and re-layouts: 4.24 us -> 2.07 us
where the time goes in v2:
time: 56.7 us; the launch traced here: 56.5 us
  Pallas kernels  54.4 us (96%)
  local copies, waits for them, and re-layouts  2.07 us (4%)
    pallas_call x1, Pallas kernels, fused(): pl.pallas_call(fused_kernel, out_shape=jax.ShapeDtypeStruct((1, ROWS, WID...  54.4 us
    unnamed x1, local copies, waits for them, and re-layouts  2.07 us

profile of v2, /device:TPU:0, one launch (start us, length us, event | category | flops | bytes accessed | tf_op | source)
XLA Modules:
  0.0 56.5 jit_solution(2424647304266878888)
XLA Ops:
  0.0 54.4 %shard_map.100 = f32[1,128,1536]{2,1,0:T(8,128)} custom-call(bf16[1,128,1536]{2,1,0:T(8,128)(2,1)} %tokens_hbm.1, bf16[1,128,1536]{2,1,0:T(8,128)(2,1)} %upstream_hbm.1, f32[1536]{0:T(1024)} %gain_hbm.1, f32[1536]{0:T(1024)} %norm_bias_hbm.1, bf16[384,2304]{1,0:T(8,128)(2,1)} %codes_hbm.1, f32[3,18]{1,0:T(4,128)} %in_scales_hbm.1, f32[2304]{0:T(1024)} %in_bias_hbm.1, ...), custom_call_target="tpu_custom_call" | custom-call | flops 2500000000 | bytes 8000000 | tf_op jit(solution)/shard_map/pallas_call | solution.py:481
  54.4 2.1 %copy.12 = f32[1,128,1536]{2,1,0:T(8,128)} copy(f32[1,128,1536]{2,1,0:T(8,128)} %shard_map.100) | data formatting | bytes 1572864
